TPU v7x, 128 devices: a whole 4x4x4 slice. The times are simulated.
128 devices in a mesh: role: 2 (over z_hi), rad: 2 (over core), lat: 32 (over x, z_lo, y).
Axes of the slice: x: 4, y: 4, z: 4 (z_hi: 2, z_lo: 2; z = z_hi * 2 + z_lo), core: 2. Of those that a mesh axis runs over, the one named last changes fastest.
Arguments:
- temp_start: float32 [32, 512, 1024], P('rad', 'lat'), may hold values from 0 to 1
- visc_ref: float32 [32, 512, 1024], P('rad', 'lat'), may hold values from 0.3 to 3
- pinned: int32 [32, 512, 1024], P('rad', 'lat'), may hold values 0 or 1
- loads: float32 [2, 32, 512, 1024], P(None, 'rad', 'lat'), may hold values from -6 to 6
Outputs:
- solutions: float32 [2, 2, 32, 512, 1024], P('role', None, 'rad', 'lat')
Inputs may be any that keep to these rules, and one draw needn't show every extreme that they name: `pinned`: 1 marks a cell held at rest in every solve.
All inputs are finite; a program needn't handle non-finite values. No bound on the sum of `pinned` on one device may be relied on, other than what follows from the above.
Results may differ from a plain program's by a relative error of at most 0.0001.
Values sent between devices are 32-bit elements; how exact they have to be, the bound alone decides.
A program may use at most 128 MiB of HBM per device.

v0:
```python
import jax
import jax.numpy as jnp
from jax import lax
from jax.experimental import pallas as pl
from jax.experimental.pallas import tpu as pltpu
from jax.sharding import PartitionSpec as P

MESH = pl.DeviceIdType.MESH
TIME_STEP = 0.1
SOFTENING = 2.0
RAYLEIGH = 8.0

K = 4
H = K + 1
N = 16
ROWS = N + H + 1
LAYERS = N + 2 * H

T, V, M, L0, L1, F4, A4, F8, G4 = range(9)
DEPTH = {T: H, V: K, M: K - 1, L0: K - 1, L1: K - 1, F4: K, A4: K, F8: H, G4: K}
LEFT, RIGHT, CORE, CORNER_LEFT, CORNER_RIGHT = range(5)


def b_masks():
    lane = lax.broadcasted_iota(jnp.int32, (1, 8, 128), 2)
    sub = lax.broadcasted_iota(jnp.int32, (1, 8, 128), 1)
    first, last = lane == 0, lane == 127
    return first, last, first & (sub == 0), last & (sub == 7)


def above(x, last):
    rolled = pltpu.roll(x, 127, 2)
    return jnp.where(last, pltpu.roll(rolled, 7, 1), rolled)


def below(x, first):
    rolled = pltpu.roll(x, 1, 2)
    return jnp.where(first, pltpu.roll(rolled, 1, 1), rolled)


def kernel(
    temp_hbm, visc_hbm, pinned_hbm, loads_hbm, out_hbm,
    temp, visc, pinned, half, coef, weight, bias, ping, pong, mid, full, mid2,
    load0, load1, bias_a, mid_a, ping_a, pong_a, full_a,
    send_sem, recv_sem, in_sem, out_sem,
):
    role, rad, lat = (lax.axis_index(name) for name in ("role", "rad", "lat"))
    peers = lax.axis_size("lat")
    left = (role, rad, lax.rem(lat + peers - 1, peers))
    right = (role, rad, lax.rem(lat + 1, peers))
    core = (role, 1 - rad, lat)
    is_forward = role == 0
    own = 1 + (H - 1) * rad

    barrier = pltpu.get_barrier_semaphore()
    for device in (left, right, core):
        pl.semaphore_signal(barrier, inc=1, device_id=device, device_id_type=MESH)

    def arriving(source, buffer, which):
        return [
            pltpu.make_async_copy(
                source.at[:, :, pl.ds(128 * j, 128)],
                buffer.at[pl.ds(own, N), pl.ds(H, N), j, :],
                in_sem.at[which, j],
            )
            for j in range(8)
        ]

    loading = [
        arriving(temp_hbm, temp, 0),
        arriving(visc_hbm, visc, 1),
        arriving(pinned_hbm, pinned, 2),
    ]
    loading_adjoint = [
        arriving(loads_hbm.at[0], load0, 3),
        arriving(loads_hbm.at[1], load1, 4),
    ]
    for copies in loading:
        for copy in copies:
            copy.start()

    @pl.when(role == 1)
    def _():
        for copies in loading_adjoint:
            for copy in copies:
                copy.start()

    outside = (ROWS - 1) * rad
    zero_row = jnp.zeros((LAYERS, 8, 128), jnp.float32)
    for buffer in (temp, half, bias, ping, pong, mid, full, mid2, bias_a, mid_a, ping_a, pong_a):
        buffer[outside] = zero_row

    def remote(buffer, which, part, rows_from, rows_to, rows, l_from, l_to, layers, device):
        return pltpu.make_async_remote_copy(
            src_ref=buffer.at[pl.ds(rows_from, rows), pl.ds(l_from, layers)],
            dst_ref=buffer.at[pl.ds(rows_to, rows), pl.ds(l_to, layers)],
            send_sem=send_sem.at[which, part],
            recv_sem=recv_sem.at[which, part],
            device_id=device,
            device_id_type=MESH,
        )

    def margins(buffer, which):
        d = DEPTH[which]
        rows_from = (1 - rad) * (1 + N - d) + rad * H
        rows_to = (1 - rad) * (H - d) + rad * (1 + N)
        return (
            remote(buffer, which, LEFT, own, own, N, H, H + N, d, left),
            remote(buffer, which, RIGHT, own, own, N, H + N - d, H - d, d, right),
            remote(buffer, which, CORE, rows_from, rows_to, d, H, H, N, core),
            remote(buffer, which, CORNER_LEFT, rows_from, rows_to, d, H - d, H - d, d, core),
            remote(buffer, which, CORNER_RIGHT, rows_from, rows_to, d, H + N, H + N, d, core),
        )

    moves = {
        which: margins(buffer, which)
        for which, buffer in (
            (T, temp), (V, visc), (M, pinned), (L0, load0), (L1, load1),
            (F4, mid), (A4, mid_a), (F8, full), (G4, mid2),
        )
    }

    def send(which):
        for part in (LEFT, RIGHT, CORE):
            moves[which][part].start()

    def have_core(*these):
        for which in these:
            moves[which][CORE].wait_recv()

    def have_sides(*these):
        for which in these:
            for part, corner in ((RIGHT, CORNER_LEFT), (LEFT, CORNER_RIGHT)):
                moves[which][part].wait_recv()
                moves[which][corner].start()
        for which in these:
            for corner in (CORNER_LEFT, CORNER_RIGHT):
                moves[which][corner].wait_recv()

    def sent(*these):
        for which in these:
            for part in range(5):
                moves[which][part].wait_send()

    first, last, bottom, top = b_masks()

    def over(extra, spans, body):
        start = own - extra * rad

        def row(i, carry):
            for low, high in spans:
                l = low
                while l < high:
                    n = min(high - l, 8)
                    body(start + i, H + l, n)
                    l += n
            return carry

        lax.fori_loop(0, N + extra, row, 0)

    def sweep(source, target, forced, extra, spans):
        def body(r, l, n):
            here = pl.ds(l, n)
            centre = source[r, here]
            total = forced[r, here] + coef[0, r, here] * source[r + 1, here]
            total = total + coef[1, r, here] * source[r - 1, here]
            total = total + coef[2, r, here] * source[r, pl.ds(l + 1, n)]
            total = total + coef[3, r, here] * source[r, pl.ds(l - 1, n)]
            total = total + coef[4, r, here] * above(centre, last)
            total = total + coef[5, r, here] * below(centre, first)
            target[r, here] = total

        over(extra, spans, body)

    def halves(field, spans):
        def body(r, l, n):
            here = pl.ds(l, n)
            half[r, here] = 0.5 * visc[r, here] * jnp.exp(-SOFTENING * field[r, here])

        over(K, spans, body)

    def couplings(field, spans, pick):
        def body(r, l, n):
            here = pl.ds(l, n)
            centre = half[r, here]
            around = (
                half[r + 1, here],
                half[r - 1, here],
                half[r, pl.ds(l + 1, n)],
                half[r, pl.ds(l - 1, n)],
                jnp.where(top, 0.0, above(centre, last)),
                jnp.where(bottom, 0.0, below(centre, first)),
            )
            diagonal = 7.0 * centre
            for other in around:
                diagonal = diagonal + other
            held = pinned[r, here].astype(jnp.float32)
            scale = (1.0 - held) / (diagonal + held)
            for i, other in enumerate(around):
                value = scale * (centre + other)
                if i == 4:
                    value = jnp.where(top, 0.0, value)
                if i == 5:
                    value = jnp.where(bottom, 0.0, value)
                coef[i, r, here] = value
            forcing = (0.5 * RAYLEIGH) * (field[r, pl.ds(l + 1, n)] - field[r, pl.ds(l - 1, n)])
            if pick:
                forcing = jnp.where(is_forward, forcing, load1[r, here])
            else:
                weight[r, here] = scale
            bias[r, here] = scale * forcing

        over(K - 1, spans, body)

    def adjoint_bias(spans):
        def body(r, l, n):
            here = pl.ds(l, n)
            bias_a[r, here] = weight[r, here] * load0[r, here]

        over(K - 1, spans, body)

    def advance(target, spans):
        def body(r, l, n):
            here, up, down = pl.ds(l, n), pl.ds(l + 1, n), pl.ds(l - 1, n)
            centre = temp[r, here]
            r_up, r_down = temp[r + 1, here], temp[r - 1, here]
            l_up, l_down = temp[r, up], temp[r, down]
            laplace = r_up + r_down + l_up + l_down
            laplace = laplace + jnp.where(top, 0.0, above(centre, last))
            laplace = laplace + jnp.where(bottom, 0.0, below(centre, first)) - 6.0 * centre
            radial = full[r, up] - full[r, down]
            lateral = full[r + 1, here] - full[r - 1, here]
            transport = 0.25 * (radial * (r_up - r_down) - lateral * (l_up - l_down))
            target[r, here] = centre + TIME_STEP * (laplace - transport)

        over(K, spans, body)

    def middle(j, shift=0):
        return ((j + shift, N - j - shift),)

    def sides(j, shift=0):
        return ((j - K, j + shift), (N - j - shift, N + K - j))

    def first_half(x, y, result, forced, spans):
        for j, source, target in ((2, forced, x), (3, x, y), (4, y, result)):
            sweep(source, target, forced, K - j, spans(j))

    def second_half(begin, x, y, result, forced, spans):
        for j, source, target in ((1, begin, x), (2, x, y), (3, y, x), (4, x, result)):
            sweep(source, target, forced, K - j, spans(j))

    def writing(buffer, which):
        return pltpu.make_async_copy(
            buffer.at[pl.ds(own, N), pl.ds(H, N)], out_hbm.at[which], out_sem.at[which]
        )

    pl.semaphore_wait(barrier, 3)
    for copies, which in zip(loading, (T, V, M)):
        for copy in copies:
            copy.wait()
        send(which)

    @pl.when(role == 1)
    def _():
        for copies, which in zip(loading_adjoint, (L0, L1)):
            for copy in copies:
                copy.wait()
            send(which)

    have_core(T, V, M)
    halves(temp, ((0, N),))
    couplings(temp, middle(1), False)
    first_half(ping, pong, mid, bias, middle)

    @pl.when(role == 1)
    def _():
        have_core(L0, L1)
        adjoint_bias(middle(1))
        first_half(ping_a, pong_a, mid_a, bias_a, middle)

    have_sides(T, V, M)
    halves(temp, ((-K, 0), (N, N + K)))
    couplings(temp, sides(1), False)
    first_half(ping, pong, mid, bias, sides)
    send(F4)

    @pl.when(role == 1)
    def _():
        have_sides(L0, L1)
        adjoint_bias(sides(1))
        first_half(ping_a, pong_a, mid_a, bias_a, sides)
        send(A4)

    have_core(F4)
    second_half(mid, ping, pong, full, bias, middle)

    @pl.when(role == 1)
    def _():
        have_core(A4)
        second_half(mid_a, ping_a, pong_a, full_a, bias_a, middle)

    have_sides(F4)
    second_half(mid, ping, pong, full, bias, sides)
    send(F8)

    @pl.when(role == 0)
    def _():
        writing(full, 0).start()

    @pl.when(role == 1)
    def _():
        have_sides(A4)
        second_half(mid_a, ping_a, pong_a, full_a, bias_a, sides)
        writing(full_a, 0).start()
        sent(A4)

    sent(F4)
    temp_next = mid
    have_core(F8)
    advance(temp_next, middle(1))
    halves(temp_next, middle(1))
    couplings(temp_next, middle(2), True)
    first_half(ping, pong, mid2, bias, lambda j: middle(j, 1))
    have_sides(F8)
    advance(temp_next, ((-K, 1), (N - 1, N + K)))
    halves(temp_next, ((-K, 1), (N - 1, N + K)))
    couplings(temp_next, sides(1, 1), True)
    first_half(ping, pong, mid2, bias, lambda j: sides(j, 1))
    send(G4)
    have_core(G4)
    final = mid_a
    second_half(mid2, ping, pong, final, bias, middle)
    have_sides(G4)
    second_half(mid2, ping, pong, final, bias, sides)
    writing(final, 1).start()
    sent(T, V, M, F8, G4)

    @pl.when(role == 1)
    def _():
        sent(L0, L1)

    writing(full, 0).wait()
    writing(final, 1).wait()


def per_device(temp_start, visc_ref, pinned, loads):
    field = pltpu.VMEM((ROWS, LAYERS, 8, 128), jnp.float32)
    scratch = [
        field, field, pltpu.VMEM((ROWS, LAYERS, 8, 128), jnp.int32), field,
        pltpu.VMEM((6, ROWS, LAYERS, 8, 128), jnp.float32),
    ] + [field] * 14 + [
        pltpu.SemaphoreType.DMA((9, 5)),
        pltpu.SemaphoreType.DMA((9, 5)),
        pltpu.SemaphoreType.DMA((5, 8)),
        pltpu.SemaphoreType.DMA((2,)),
    ]
    result = pl.pallas_call(
        kernel,
        out_shape=jax.ShapeDtypeStruct((2, N, N, 8, 128), jnp.float32),
        in_specs=[pl.BlockSpec(memory_space=pl.ANY)] * 4,
        out_specs=pl.BlockSpec(memory_space=pl.ANY),
        scratch_shapes=scratch,
        compiler_params=pltpu.CompilerParams(
            collective_id=0, has_side_effects=True, vmem_limit_bytes=60 * 1024 * 1024
        ),
    )(temp_start, visc_ref, pinned, loads)
    return result.reshape(1, 2, N, N, 1024)


def solution(mesh):
    in_specs = (
        P("rad", "lat", None),
        P("rad", "lat", None),
        P("rad", "lat", None),
        P(None, "rad", "lat", None),
    )
    out_specs = P("role", None, "rad", "lat", None)
    return jax.shard_map(
        per_device, mesh=mesh, in_specs=in_specs, out_specs=out_specs, check_vma=False
    )
```

profile of v0, /device:TPU:65, one launch (start us, length us, event | category | flops | bytes accessed | tf_op | source)
XLA Modules:
  0.0 112.2 jit_solution(4162974564011194963)
XLA Ops:
  0.0 109.5 %shard_map.46 = f32[2,16,16,8,128]{4,3,2,1,0:T(8,128)} custom-call(f32[16,16,1024]{2,1,0:T(8,128)} %temp_hbm.1, f32[16,16,1024]{2,1,0:T(8,128)} %visc_hbm.1, s32[16,16,1024]{2,1,0:T(8,128)} %pinned_hbm.1, f32[2,16,16,1024]{3,2,1,0:T(8,128)} %loads_hbm.1), custom_call_target="tpu_custom_call" | custom-call | tf_op jit(solution)/shard_map/pallas_call | solution.py:357
  109.5 2.7 %reshape.3 = f32[1,2,16,16,1024]{4,3,2,1,0:T(8,128)} reshape(f32[2,16,16,8,128]{4,3,2,1,0:T(8,128)} %shard_map.46) | data formatting | bytes 4194304 | tf_op jit(solution)/shard_map/reshape | solution.py:367
where the time goes:
time: 112 us
  Pallas kernels  109 us (97%)
  local copies, waits for them, and re-layouts  2.7 us (2%)
    pallas_call x1, Pallas kernels, per_device(): pl.pallas_call(kernel, out_shape=jax.ShapeDtypeStruct((2, N, N, 8, 128),...  109 us
    reshape x1, local copies, waits for them, and re-layouts, per_device(): return result.reshape(1, 2, N, N, 1024)  2.7 us

commit v1 on v0

--- a/solution.py
+++ b/solution.py
@@ -145,18 +145,23 @@
     first, last, bottom, top = b_masks()
 
     def over(extra, spans, body):
+        extra = (0, 2, 2, 4, 4)[extra]
+        group = (N + extra) // 2
         start = own - extra * rad
 
-        def row(i, carry):
-            for low, high in spans:
-                l = low
-                while l < high:
-                    n = min(high - l, 8)
-                    body(start + i, H + l, n)
-                    l += n
-            return carry
-
-        lax.fori_loop(0, N + extra, row, 0)
+        def rows(g, carry):
+            def row(i, inner):
+                for low, high in spans:
+                    l = low
+                    while l < high:
+                        n = min(high - l, 8)
+                        body(start + g * group + i, H + l, n)
+                        l += n
+                return inner
+
+            return lax.fori_loop(0, group, row, carry, unroll=True)
+
+        lax.fori_loop(0, 2, rows, 0)
 
     def sweep(source, target, forced, extra, spans):
         def body(r, l, n):

time: 112 us -> 76.6 us (0.68)
  Pallas kernels: 109 us -> 73.4 us
    pallas_call x1, Pallas kernels: 109 us -> 73.4 us  [per_device(): pl.pallas_call(kernel, out_shape=jax.ShapeDtypeStruct((2, N, N, 8, 128),...]
where the time goes in v1:
time: 76.6 us; the launch traced here: 76.1 us
  Pallas kernels  73.4 us (96%)
  local copies, waits for them, and re-layouts  2.7 us (4%)
    pallas_call x1, Pallas kernels, per_device(): pl.pallas_call(kernel, out_shape=jax.ShapeDtypeStruct((2, N, N, 8, 128),...  73.4 us
    reshape x1, local copies, waits for them, and re-layouts, per_device(): return result.reshape(1, 2, N, N, 1024)  2.7 us

profile of v1, /device:TPU:65, one launch (start us, length us, event | category | flops | bytes accessed | tf_op | source)
XLA Modules:
  0.0 76.1 jit_solution(13800123177865093141)
XLA Ops:
  0.0 73.4 %shard_map.46 = f32[2,16,16,8,128]{4,3,2,1,0:T(8,128)} custom-call(f32[16,16,1024]{2,1,0:T(8,128)} %temp_hbm.1, f32[16,16,1024]{2,1,0:T(8,128)} %visc_hbm.1, s32[16,16,1024]{2,1,0:T(8,128)} %pinned_hbm.1, f32[2,16,16,1024]{3,2,1,0:T(8,128)} %loads_hbm.1), custom_call_target="tpu_custom_call" | custom-call | tf_op jit(solution)/shard_map/pallas_call | solution.py:362
  73.4 2.7 %reshape.3 = f32[1,2,16,16,1024]{4,3,2,1,0:T(8,128)} reshape(f32[2,16,16,8,128]{4,3,2,1,0:T(8,128)} %shard_map.46) | data formatting | bytes 4194304 | tf_op jit(solution)/shard_map/reshape | solution.py:372

commit v2 on v1

v2 whole, which is shorter than its diff:
```python
import jax
import jax.numpy as jnp
from jax import lax
from jax.experimental import pallas as pl
from jax.experimental.pallas import tpu as pltpu
from jax.sharding import PartitionSpec as P

MESH = pl.DeviceIdType.MESH
TIME_STEP = 0.1
SOFTENING = 2.0
RAYLEIGH = 8.0

K = 4
H = K + 1
N = 16
ROWS = N + H + 1

T, V, M, L0, L1, F4, A4, F8, G4 = range(9)
DEPTH = {T: H, V: K, M: K - 1, L0: K - 1, L1: K - 1, F4: K, A4: K, F8: H, G4: K}
STEPS = (12, 8, 4, 0)
WHOLE = (0,)
CHUNKS = {T: (11, 8, 4, 0), V: STEPS, M: STEPS, L0: WHOLE, L1: WHOLE, F4: STEPS, A4: WHOLE, F8: STEPS, G4: STEPS}
CORE, CORNER_LEFT, CORNER_RIGHT, LEFT, RIGHT = 0, 1, 2, 3, 7


def b_masks():
    lane = lax.broadcasted_iota(jnp.int32, (1, 8, 128), 2)
    sub = lax.broadcasted_iota(jnp.int32, (1, 8, 128), 1)
    first, last = lane == 0, lane == 127
    return first, last, first & (sub == 0), last & (sub == 7)


def above(x, last):
    rolled = pltpu.roll(x, 127, 2)
    return jnp.where(last, pltpu.roll(rolled, 7, 1), rolled)


def below(x, first):
    rolled = pltpu.roll(x, 1, 2)
    return jnp.where(first, pltpu.roll(rolled, 1, 1), rolled)


class Field:
    def __init__(self, ref, margin):
        self.ref, self.margin = ref, margin

    def get(self, r, l, n):
        return self.ref[r, pl.ds(self.margin + l, n)]

    def put(self, r, l, value):
        self.ref[r, pl.ds(self.margin + l, value.shape[0])] = value

    def view(self, r, rows, l, layers):
        return self.ref.at[pl.ds(r, rows), pl.ds(self.margin + l, layers)]


MARGINS = (
    ("temp", H), ("visc", K), ("pinned", 3), ("half", K), ("weight", 3), ("bias", 3), ("ping", 3), ("pong", 3),
    ("mid", K), ("full", H), ("mid2", K), ("load0", 3), ("load1", 3), ("bias_a", 3), ("mid_a", K),
    ("ping_a", 3), ("pong_a", 3), ("full_a", 0),
)


def kernel(temp_hbm, visc_hbm, pinned_hbm, loads_hbm, out_hbm, *scratch):
    fields = {name: Field(ref, margin) for (name, margin), ref in zip(MARGINS, scratch)}
    coef1, coef2, send_sem, recv_sem, in_sem, out_sem = scratch[len(MARGINS):]
    temp, visc, pinned, half, weight, bias, ping, pong, mid, full, mid2 = (
        fields[name] for name, _ in MARGINS[:11]
    )
    load0, load1, bias_a, mid_a, ping_a, pong_a, full_a = (fields[name] for name, _ in MARGINS[11:])

    role, rad, lat = (lax.axis_index(name) for name in ("role", "rad", "lat"))
    peers = lax.axis_size("lat")
    left = (role, rad, lax.rem(lat + peers - 1, peers))
    right = (role, rad, lax.rem(lat + 1, peers))
    core = (role, 1 - rad, lat)
    is_forward = role == 0
    own = 1 + (H - 1) * rad

    barrier = pltpu.get_barrier_semaphore()
    for device in (left, right, core):
        pl.semaphore_signal(barrier, inc=1, device_id=device, device_id_type=MESH)

    def arriving(source, field, which):
        return [
            pltpu.make_async_copy(
                source.at[:, :, pl.ds(128 * j, 128)],
                field.ref.at[pl.ds(own, N), pl.ds(field.margin, N), j, :],
                in_sem.at[which, j],
            )
            for j in range(8)
        ]

    loading = [
        arriving(temp_hbm, temp, 0),
        arriving(visc_hbm, visc, 1),
        arriving(pinned_hbm, pinned, 2),
    ]
    loading_adjoint = [
        arriving(loads_hbm.at[1], load1, 3),
        arriving(loads_hbm.at[0], load0, 4),
    ]
    for copies in loading:
        for copy in copies:
            copy.start()

    @pl.when(role == 1)
    def _():
        for copies in loading_adjoint:
            for copy in copies:
                copy.start()

    outside = (ROWS - 1) * rad
    for field in (temp, half, bias, ping, pong, mid, full, mid2, bias_a, mid_a, ping_a, pong_a):
        field.ref[outside] = jnp.zeros((N + 2 * field.margin, 8, 128), jnp.float32)

    def first_row(low, high):
        return own + (1 - rad) * low + rad * (N - high)

    def remote(field, which, part, rows_from, rows_to, rows, l_from, l_to, layers, device):
        return pltpu.make_async_remote_copy(
            src_ref=field.view(rows_from, rows, l_from, layers),
            dst_ref=field.view(rows_to, rows, l_to, layers),
            send_sem=send_sem.at[which, part],
            recv_sem=recv_sem.at[which, part],
            device_id=device,
            device_id_type=MESH,
        )

    def margins(field, which):
        d = DEPTH[which]
        rows_from = (1 - rad) * (1 + N - d) + rad * H
        rows_to = (1 - rad) * (H - d) + rad * (1 + N)
        parts = {
            CORE: remote(field, which, CORE, rows_from, rows_to, d, 0, 0, N, core),
            CORNER_LEFT: remote(field, which, CORNER_LEFT, rows_from, rows_to, d, -d, -d, d, core),
            CORNER_RIGHT: remote(field, which, CORNER_RIGHT, rows_from, rows_to, d, N, N, d, core),
        }
        high = N
        for i, low in enumerate(CHUNKS[which]):
            row, rows = first_row(low, high), high - low
            parts[LEFT + i] = remote(field, which, LEFT + i, row, row, rows, 0, N, d, left)
            parts[RIGHT + i] = remote(field, which, RIGHT + i, row, row, rows, N - d, -d, d, right)
            high = low
        return parts

    moves = {
        which: margins(field, which)
        for which, field in (
            (T, temp), (V, visc), (M, pinned), (L0, load0), (L1, load1),
            (F4, mid), (A4, mid_a), (F8, full), (G4, mid2),
        )
    }

    def send_core(which):
        moves[which][CORE].start()

    def send_chunk(which, i):
        moves[which][LEFT + i].start()
        moves[which][RIGHT + i].start()

    def have_core(*these):
        for which in these:
            moves[which][CORE].wait_recv()

    def have_chunk(i, *these):
        for which in these:
            moves[which][LEFT + i].wait_recv()
            moves[which][RIGHT + i].wait_recv()

    def send_corners(*these):
        for which in these:
            moves[which][CORNER_LEFT].start()
            moves[which][CORNER_RIGHT].start()

    def have_corners(*these):
        for which in these:
            moves[which][CORNER_LEFT].wait_recv()
            moves[which][CORNER_RIGHT].wait_recv()

    def have_sides(which):
        have_chunk(0, which)
        send_corners(which)
        have_corners(which)

    def sent(*these):
        for which in these:
            for move in moves[which].values():
                move.wait_send()

    first, last, bottom, top = b_masks()

    def over(low, high, spans, body):
        if high - low <= 11:
            groups = 1
        else:
            groups = 2
            high += (high - low) % 2
        group = (high - low) // groups
        start = first_row(low, high)

        def rows(g, carry):
            def row(i, inner):
                for begin, end in spans:
                    l = begin
                    while l < end:
                        n = min(end - l, 8)
                        body(start + g * group + i, l, n)
                        l += n
                return inner

            return lax.fori_loop(0, group, row, carry, unroll=True)

        if groups == 1:
            rows(0, 0)
        else:
            lax.fori_loop(0, groups, rows, 0)

    def sweep(source, target, forced, coef, spans):
        def body(r, l, n):
            here = pl.ds(3 + l, n)
            centre = source.get(r, l, n)
            total = forced.get(r, l, n) + coef[0, r, here] * source.get(r + 1, l, n)
            total = total + coef[1, r, here] * source.get(r - 1, l, n)
            total = total + coef[2, r, here] * source.get(r, l + 1, n)
            total = total + coef[3, r, here] * source.get(r, l - 1, n)
            total = total + coef[4, r, here] * above(centre, last)
            total = total + coef[5, r, here] * below(centre, first)
            target.put(r, l, total)

        return lambda low, high: over(low, high, spans, body)

    def halves(field, spans):
        def body(r, l, n):
            half.put(r, l, 0.5 * visc.get(r, l, n) * jnp.exp(-SOFTENING * field.get(r, l, n)))

        return lambda low, high: over(low, high, spans, body)

    def couplings(field, coef, spans, pick):
        def body(r, l, n):
            here = pl.ds(3 + l, n)
            centre = half.get(r, l, n)
            around = (
                half.get(r + 1, l, n),
                half.get(r - 1, l, n),
                half.get(r, l + 1, n),
                half.get(r, l - 1, n),
                jnp.where(top, 0.0, above(centre, last)),
                jnp.where(bottom, 0.0, below(centre, first)),
            )
            diagonal = 7.0 * centre
            for other in around:
                diagonal = diagonal + other
            held = pinned.get(r, l, n).astype(jnp.float32)
            scale = (1.0 - held) / (diagonal + held)
            for i, other in enumerate(around):
                value = scale * (centre + other)
                if i == 4:
                    value = jnp.where(top, 0.0, value)
                if i == 5:
                    value = jnp.where(bottom, 0.0, value)
                coef[i, r, here] = value
            forcing = (0.5 * RAYLEIGH) * (field.get(r, l + 1, n) - field.get(r, l - 1, n))
            if pick:
                forcing = jnp.where(is_forward, forcing, load1.get(r, l, n))
            else:
                weight.put(r, l, scale)
            bias.put(r, l, scale * forcing)

        return lambda low, high: over(low, high, spans, body)

    def adjoint_bias(spans):
        def body(r, l, n):
            bias_a.put(r, l, weight.get(r, l, n) * load0.get(r, l, n))

        return lambda low, high: over(low, high, spans, body)

    def advance(target, spans):
        def body(r, l, n):
            centre = temp.get(r, l, n)
            r_up, r_down = temp.get(r + 1, l, n), temp.get(r - 1, l, n)
            l_up, l_down = temp.get(r, l + 1, n), temp.get(r, l - 1, n)
            laplace = r_up + r_down + l_up + l_down
            laplace = laplace + jnp.where(top, 0.0, above(centre, last))
            laplace = laplace + jnp.where(bottom, 0.0, below(centre, first)) - 6.0 * centre
            radial = full.get(r, l + 1, n) - full.get(r, l - 1, n)
            lateral = full.get(r + 1, l, n) - full.get(r - 1, l, n)
            transport = 0.25 * (radial * (r_up - r_down) - lateral * (l_up - l_down))
            target.put(r, l, centre + TIME_STEP * (laplace - transport))

        return lambda low, high: over(low, high, spans, body)

    def middle(j, shift=0):
        return ((j + shift, N - j - shift),)

    def sides(j, shift=0):
        return ((j - K, j + shift), (N - j - shift, N + K - j))

    def first_half(x, y, result, forced, coef, spans, lag):
        return [
            (sweep(source, target, forced, coef, spans(j)), lag + j, N + K - j)
            for j, source, target in ((2, forced, x), (3, x, y), (4, y, result))
        ]

    def second_half(begin, x, y, result, forced, coef, spans):
        return [
            (sweep(source, target, forced, coef, spans(j)), j, N + K - j)
            for j, source, target in ((1, begin, x), (2, x, y), (3, y, x), (4, x, result))
        ]

    def all_rows(stage):
        for work, _, high in stage:
            work(0, high)

    def wave(stage, arrive, leave):
        highs = [high for _, _, high in stage]
        for i, low in enumerate(STEPS):
            arrive(i)
            if i == 0:
                continue
            for place, (work, lag, _) in enumerate(stage):
                begin = min(low + lag, highs[place]) if low else 0
                if begin < highs[place]:
                    work(begin, highs[place])
                    highs[place] = begin
            leave(i)

    def writing(field, which, part, low, high):
        row = first_row(low, high)
        return pltpu.make_async_copy(
            field.view(row, high - low, 0, N),
            out_hbm.at[which, pl.ds(row - own, high - low)],
            out_sem.at[which, part],
        )

    for copies in loading:
        for copy in copies:
            copy.wait()
    pl.semaphore_wait(barrier, 3)
    for i in range(len(STEPS)):
        for which in (T, V, M):
            send_chunk(which, i)
        if i == 0:
            for which in (T, V, M):
                send_core(which)

    @pl.when(role == 1)
    def _():
        for copies in loading_adjoint:
            for copy in copies:
                copy.wait()
        send_chunk(L1, 0)
        send_core(L0)
        send_core(L1)

    have_core(T, V, M)
    all_rows(
        [(halves(temp, ((0, N),)), 0, N + K), (couplings(temp, coef1, middle(1), False), 1, N + K - 1)]
        + first_half(ping, pong, mid, bias, coef1, middle, 0)
    )

    def inputs_arrive(i):
        have_chunk(i, T, V, M)
        if i == 0:
            send_corners(T, V, M)
        if i == 1:
            have_corners(T, V, M)

    def leave_four(which):
        def leave(i):
            if i == 1:
                send_chunk(which, 0)
                send_core(which)
            if i == 2:
                send_chunk(which, 1)
            if i == 3:
                send_chunk(which, 2)
                send_chunk(which, 3)

        return leave

    wave(
        [(halves(temp, ((-K, 0), (N, N + K))), 0, N + K), (couplings(temp, coef1, sides(1), False), 1, N + K - 1)]
        + first_half(ping, pong, mid, bias, coef1, sides, 0),
        inputs_arrive,
        leave_four(F4),
    )

    @pl.when(role == 1)
    def _():
        send_chunk(L0, 0)

    have_core(F4)
    all_rows(second_half(mid, ping, pong, full, bias, coef1, middle))

    @pl.when(role == 1)
    def _():
        have_core(L0, L1)
        all_rows(
            [(adjoint_bias(middle(1)), 0, N + K - 1)]
            + first_half(ping_a, pong_a, mid_a, bias_a, coef1, middle, 0)
        )
        have_sides(L1)

    def potential_arrives(which):
        def arrive(i):
            have_chunk(i, which)
            if i == 0:
                send_corners(which)
            if i == 1:
                have_corners(which)

        return arrive

    def leave_full(i):
        if i == 1:
            send_chunk(F8, 0)
        if i == 2:
            send_chunk(F8, 1)
            send_core(F8)
        if i == 3:
            send_chunk(F8, 2)
            send_chunk(F8, 3)

    wave(second_half(mid, ping, pong, full, bias, coef1, sides), potential_arrives(F4), leave_full)

    @pl.when(role == 0)
    def _():
        writing(full, 0, 0, 0, N).start()

    @pl.when(role == 1)
    def _():
        have_sides(L0)
        all_rows(
            [(adjoint_bias(sides(1)), 0, N + K - 1)]
            + first_half(ping_a, pong_a, mid_a, bias_a, coef1, sides, 0)
        )
        send_chunk(A4, 0)
        send_core(A4)

    sent(F4)
    temp_next = mid
    have_core(F8)
    all_rows(
        [
            (advance(temp_next, middle(1)), 0, N + K),
            (halves(temp_next, middle(1)), 0, N + K),
            (couplings(temp_next, coef2, middle(2), True), 0, N + K - 1),
        ]
        + first_half(ping, pong, mid2, bias, coef2, lambda j: middle(j, 1), 0)
    )

    def full_arrives(i):
        have_chunk(i, F8)
        if i == 1:
            send_corners(F8)
            have_corners(F8)

    def leave_next(i):
        if i == 2:
            send_chunk(G4, 0)
            send_core(G4)
        if i == 3:
            send_chunk(G4, 1)
            send_chunk(G4, 2)
            send_chunk(G4, 3)

    wave(
        [
            (advance(temp_next, ((-K, 1), (N - 1, N + K))), 1, N + K),
            (halves(temp_next, ((-K, 1), (N - 1, N + K))), 1, N + K),
            (couplings(temp_next, coef2, sides(1, 1), True), 2, N + K - 1),
        ]
        + first_half(ping, pong, mid2, bias, coef2, lambda j: sides(j, 1), 1),
        full_arrives,
        leave_next,
    )
    final = temp
    sent(T, V, M)
    have_core(G4)
    all_rows(second_half(mid2, ping, pong, final, bias, coef2, middle))

    @pl.when(role == 1)
    def _():
        have_core(A4)
        all_rows(second_half(mid_a, ping_a, pong_a, full_a, bias_a, coef1, middle))
        have_sides(A4)
        all_rows(second_half(mid_a, ping_a, pong_a, full_a, bias_a, coef1, sides))
        writing(full_a, 0, 0, 0, N).start()

    def leave_final(i):
        if i == 2:
            writing(final, 1, 0, 8, N).start()
        if i == 3:
            writing(final, 1, 1, 0, 8).start()

    wave(second_half(mid2, ping, pong, final, bias, coef2, sides), potential_arrives(G4), leave_final)
    sent(F8, G4)

    @pl.when(role == 1)
    def _():
        sent(L0, L1, A4)

    writing(full, 0, 0, 0, N).wait()
    writing(final, 1, 0, 8, N).wait()
    writing(final, 1, 1, 0, 8).wait()


def per_device(temp_start, visc_ref, pinned, loads):
    def block(margin, dtype=jnp.float32, lead=()):
        return pltpu.VMEM(lead + (ROWS, N + 2 * margin, 8, 128), dtype)

    scratch = [block(margin, jnp.int32 if name == "pinned" else jnp.float32) for name, margin in MARGINS]
    scratch += [block(3, lead=(6,)), block(3, lead=(6,))]
    scratch += [
        pltpu.SemaphoreType.DMA((9, 11)),
        pltpu.SemaphoreType.DMA((9, 11)),
        pltpu.SemaphoreType.DMA((5, 8)),
        pltpu.SemaphoreType.DMA((2, 2)),
    ]
    result = pl.pallas_call(
        kernel,
        out_shape=jax.ShapeDtypeStruct((2, N, N, 8, 128), jnp.float32),
        in_specs=[pl.BlockSpec(memory_space=pl.ANY)] * 4,
        out_specs=pl.BlockSpec(memory_space=pl.ANY),
        scratch_shapes=scratch,
        compiler_params=pltpu.CompilerParams(
            collective_id=0, has_side_effects=True, vmem_limit_bytes=60 * 1024 * 1024
        ),
    )(temp_start, visc_ref, pinned, loads)
    return result.reshape(1, 2, N, N, 1024)


def solution(mesh):
    in_specs = (
        P("rad", "lat", None),
        P("rad", "lat", None),
        P("rad", "lat", None),
        P(None, "rad", "lat", None),
    )
    out_specs = P("role", None, "rad", "lat", None)
    return jax.shard_map(
        per_device, mesh=mesh, in_specs=in_specs, out_specs=out_specs, check_vma=False
    )
```

time: 76.6 us -> 68.2 us (0.89)
  Pallas kernels: 73.4 us -> 65.3 us
    pallas_call x1, Pallas kernels: 73.4 us -> 65.3 us  [per_device(): pl.pallas_call(kernel, out_shape=jax.ShapeDtypeStruct((2, N, N, 8, 128),...]
where the time goes in v2:
time: 68.2 us; the launch traced here: 68 us
  Pallas kernels  65.3 us (96%)
  local copies, waits for them, and re-layouts  2.7 us (4%)
    pallas_call x1, Pallas kernels, per_device(): pl.pallas_call(kernel, out_shape=jax.ShapeDtypeStruct((2, N, N, 8, 128),...  65.3 us
    reshape x1, local copies, waits for them, and re-layouts, per_device(): return result.reshape(1, 2, N, N, 1024)  2.7 us

profile of v2, /device:TPU:65, one launch (start us, length us, event | category | flops | bytes accessed | tf_op | source)
XLA Modules:
  0.0 68.0 jit_solution(40890449059567728)
XLA Ops:
  0.0 65.3 %shard_map.46 = f32[2,16,16,8,128]{4,3,2,1,0:T(8,128)} custom-call(f32[16,16,1024]{2,1,0:T(8,128)} %temp_hbm.1, f32[16,16,1024]{2,1,0:T(8,128)} %visc_hbm.1, s32[16,16,1024]{2,1,0:T(8,128)} %pinned_hbm.1, f32[2,16,16,1024]{3,2,1,0:T(8,128)} %loads_hbm.1), custom_call_target="tpu_custom_call" | custom-call | tf_op jit(solution)/shard_map/pallas_call | solution.py:521
  65.3 2.7 %reshape.3 = f32[1,2,16,16,1024]{4,3,2,1,0:T(8,128)} reshape(f32[2,16,16,8,128]{4,3,2,1,0:T(8,128)} %shard_map.46) | data formatting | bytes 4194304 | tf_op jit(solution)/shard_map/reshape | solution.py:531

commit v3 on v2

--- a/solution.py
+++ b/solution.py
@@ -15,11 +15,12 @@
 N = 16
 ROWS = N + H + 1
 
-T, V, M, L0, L1, F4, A4, F8, G4 = range(9)
-DEPTH = {T: H, V: K, M: K - 1, L0: K - 1, L1: K - 1, F4: K, A4: K, F8: H, G4: K}
-STEPS = (12, 8, 4, 0)
+T, V, M, L0, L1, F4, A4, F8, G4, FAR = range(10)
+DEPTH = {T: K, V: K, M: K - 1, L0: K - 1, L1: K - 1, F4: K, A4: K, F8: H, G4: K, FAR: 1}
+STEPS = (12, 6, 2, 0)
+LATER = (12, 7, 2, 0)
 WHOLE = (0,)
-CHUNKS = {T: (11, 8, 4, 0), V: STEPS, M: STEPS, L0: WHOLE, L1: WHOLE, F4: STEPS, A4: WHOLE, F8: STEPS, G4: STEPS}
+CHUNKS = {T: (11, 6, 2, 0), V: STEPS, M: STEPS, F4: STEPS, F8: STEPS, G4: LATER}
 CORE, CORNER_LEFT, CORNER_RIGHT, LEFT, RIGHT = 0, 1, 2, 3, 7
 
 
@@ -97,8 +98,8 @@
         arriving(pinned_hbm, pinned, 2),
     ]
     loading_adjoint = [
-        arriving(loads_hbm.at[1], load1, 3),
-        arriving(loads_hbm.at[0], load0, 4),
+        arriving(loads_hbm.at[0], load0, 3),
+        arriving(loads_hbm.at[1], load1, 4),
     ]
     for copies in loading:
         for copy in copies:
@@ -129,18 +130,22 @@
 
     def margins(field, which):
         d = DEPTH[which]
-        rows_from = (1 - rad) * (1 + N - d) + rad * H
-        rows_to = (1 - rad) * (H - d) + rad * (1 + N)
+        rows = H if which in (T, FAR) else d
+        skip = K if which == FAR else 0
+        rows_from = (1 - rad) * (1 + N - rows) + rad * H
+        rows_to = (1 - rad) * (H - rows) + rad * (1 + N)
+        before, after = -skip - d, N + skip
         parts = {
-            CORE: remote(field, which, CORE, rows_from, rows_to, d, 0, 0, N, core),
-            CORNER_LEFT: remote(field, which, CORNER_LEFT, rows_from, rows_to, d, -d, -d, d, core),
-            CORNER_RIGHT: remote(field, which, CORNER_RIGHT, rows_from, rows_to, d, N, N, d, core),
+            CORNER_LEFT: remote(field, which, CORNER_LEFT, rows_from, rows_to, rows, before, before, d, core),
+            CORNER_RIGHT: remote(field, which, CORNER_RIGHT, rows_from, rows_to, rows, after, after, d, core),
         }
+        if which != FAR:
+            parts[CORE] = remote(field, which, CORE, rows_from, rows_to, rows, 0, 0, N, core)
         high = N
-        for i, low in enumerate(CHUNKS[which]):
+        for i, low in enumerate(CHUNKS.get(which, WHOLE)):
             row, rows = first_row(low, high), high - low
-            parts[LEFT + i] = remote(field, which, LEFT + i, row, row, rows, 0, N, d, left)
-            parts[RIGHT + i] = remote(field, which, RIGHT + i, row, row, rows, N - d, -d, d, right)
+            parts[LEFT + i] = remote(field, which, LEFT + i, row, row, rows, skip, after, d, left)
+            parts[RIGHT + i] = remote(field, which, RIGHT + i, row, row, rows, N - skip - d, before, d, right)
             high = low
         return parts
 
@@ -148,7 +153,7 @@
         which: margins(field, which)
         for which, field in (
             (T, temp), (V, visc), (M, pinned), (L0, load0), (L1, load1),
-            (F4, mid), (A4, mid_a), (F8, full), (G4, mid2),
+            (F4, mid), (A4, mid_a), (F8, full), (G4, mid2), (FAR, temp),
         )
     }
 
@@ -191,7 +196,7 @@
     first, last, bottom, top = b_masks()
 
     def over(low, high, spans, body):
-        if high - low <= 11:
+        if high - low <= 11 or (high - low) % 2 and high == N + K:
             groups = 1
         else:
             groups = 2
@@ -312,9 +317,9 @@
         for work, _, high in stage:
             work(0, high)
 
-    def wave(stage, arrive, leave):
+    def wave(stage, arrive, leave, steps=STEPS):
         highs = [high for _, _, high in stage]
-        for i, low in enumerate(STEPS):
+        for i, low in enumerate(steps):
             arrive(i)
             if i == 0:
                 continue
@@ -349,7 +354,7 @@
         for copies in loading_adjoint:
             for copy in copies:
                 copy.wait()
-        send_chunk(L1, 0)
+        send_chunk(L0, 0)
         send_core(L0)
         send_core(L1)
 
@@ -386,9 +391,11 @@
         leave_four(F4),
     )
 
-    @pl.when(role == 1)
-    def _():
-        send_chunk(L0, 0)
+    send_chunk(FAR, 0)
+
+    @pl.when(role == 1)
+    def _():
+        send_chunk(L1, 0)
 
     have_core(F4)
     all_rows(second_half(mid, ping, pong, full, bias, coef1, middle))
@@ -400,7 +407,11 @@
             [(adjoint_bias(middle(1)), 0, N + K - 1)]
             + first_half(ping_a, pong_a, mid_a, bias_a, coef1, middle, 0)
         )
-        have_sides(L1)
+        have_sides(L0)
+        all_rows(
+            [(adjoint_bias(sides(1)), 0, N + K - 1)]
+            + first_half(ping_a, pong_a, mid_a, bias_a, coef1, sides, 0)
+        )
 
     def potential_arrives(which):
         def arrive(i):
@@ -415,9 +426,9 @@
     def leave_full(i):
         if i == 1:
             send_chunk(F8, 0)
+            send_core(F8)
         if i == 2:
             send_chunk(F8, 1)
-            send_core(F8)
         if i == 3:
             send_chunk(F8, 2)
             send_chunk(F8, 3)
@@ -430,11 +441,6 @@
 
     @pl.when(role == 1)
     def _():
-        have_sides(L0)
-        all_rows(
-            [(adjoint_bias(sides(1)), 0, N + K - 1)]
-            + first_half(ping_a, pong_a, mid_a, bias_a, coef1, sides, 0)
-        )
         send_chunk(A4, 0)
         send_core(A4)
 
@@ -449,6 +455,11 @@
         ]
         + first_half(ping, pong, mid2, bias, coef2, lambda j: middle(j, 1), 0)
     )
+    have_sides(FAR)
+
+    @pl.when(role == 1)
+    def _():
+        have_sides(L1)
 
     def full_arrives(i):
         have_chunk(i, F8)
@@ -457,11 +468,12 @@
             have_corners(F8)
 
     def leave_next(i):
-        if i == 2:
+        if i == 1:
             send_chunk(G4, 0)
             send_core(G4)
+        if i == 2:
+            send_chunk(G4, 1)
         if i == 3:
-            send_chunk(G4, 1)
             send_chunk(G4, 2)
             send_chunk(G4, 3)
 
@@ -476,7 +488,7 @@
         leave_next,
     )
     final = temp
-    sent(T, V, M)
+    sent(T, V, M, FAR)
     have_core(G4)
     all_rows(second_half(mid2, ping, pong, final, bias, coef2, middle))
 
@@ -490,11 +502,11 @@
 
     def leave_final(i):
         if i == 2:
-            writing(final, 1, 0, 8, N).start()
+            writing(final, 1, 0, 6, N).start()
         if i == 3:
-            writing(final, 1, 1, 0, 8).start()
-
-    wave(second_half(mid2, ping, pong, final, bias, coef2, sides), potential_arrives(G4), leave_final)
+            writing(final, 1, 1, 0, 6).start()
+
+    wave(second_half(mid2, ping, pong, final, bias, coef2, sides), potential_arrives(G4), leave_final, LATER)
     sent(F8, G4)
 
     @pl.when(role == 1)
@@ -502,8 +514,8 @@
         sent(L0, L1, A4)
 
     writing(full, 0, 0, 0, N).wait()
-    writing(final, 1, 0, 8, N).wait()
-    writing(final, 1, 1, 0, 8).wait()
+    writing(final, 1, 0, 6, N).wait()
+    writing(final, 1, 1, 0, 6).wait()
 
 
 def per_device(temp_start, visc_ref, pinned, loads):
@@ -513,8 +525,8 @@
     scratch = [block(margin, jnp.int32 if name == "pinned" else jnp.float32) for name, margin in MARGINS]
     scratch += [block(3, lead=(6,)), block(3, lead=(6,))]
     scratch += [
-        pltpu.SemaphoreType.DMA((9, 11)),
-        pltpu.SemaphoreType.DMA((9, 11)),
+        pltpu.SemaphoreType.DMA((10, 11)),
+        pltpu.SemaphoreType.DMA((10, 11)),
         pltpu.SemaphoreType.DMA((5, 8)),
         pltpu.SemaphoreType.DMA((2, 2)),
     ]

time: 68.2 us -> 67.2 us (0.985)
  Pallas kernels: 65.3 us -> 64.3 us
    pallas_call x1, Pallas kernels: 65.3 us -> 64.3 us  [per_device(): pl.pallas_call(kernel, out_shape=jax.ShapeDtypeStruct((2, N, N, 8, 128),...]
where the time goes in v3:
time: 67.2 us; the launch traced here: 67.1 us
  Pallas kernels  64.3 us (96%)
  local copies, waits for them, and re-layouts  2.7 us (4%)
    pallas_call x1, Pallas kernels, per_device(): pl.pallas_call(kernel, out_shape=jax.ShapeDtypeStruct((2, N, N, 8, 128),...  64.3 us
    reshape x1, local copies, waits for them, and re-layouts, per_device(): return result.reshape(1, 2, N, N, 1024)  2.7 us

profile of v3, /device:TPU:65, one launch (start us, length us, event | category | flops | bytes accessed | tf_op | source)
XLA Modules:
  0.0 67.1 jit_solution(2571725428590864706)
XLA Ops:
  0.0 64.3 %shard_map.46 = f32[2,16,16,8,128]{4,3,2,1,0:T(8,128)} custom-call(f32[16,16,1024]{2,1,0:T(8,128)} %temp_hbm.1, f32[16,16,1024]{2,1,0:T(8,128)} %visc_hbm.1, s32[16,16,1024]{2,1,0:T(8,128)} %pinned_hbm.1, f32[2,16,16,1024]{3,2,1,0:T(8,128)} %loads_hbm.1), custom_call_target="tpu_custom_call" | custom-call | tf_op jit(solution)/shard_map/pallas_call | solution.py:533
  64.4 2.7 %reshape.3 = f32[1,2,16,16,1024]{4,3,2,1,0:T(8,128)} reshape(f32[2,16,16,8,128]{4,3,2,1,0:T(8,128)} %shard_map.46) | data formatting | bytes 4194304 | tf_op jit(solution)/shard_map/reshape | solution.py:543

commit v4 on v3

--- a/solution.py
+++ b/solution.py
@@ -496,11 +496,17 @@
     def _():
         have_core(A4)
         all_rows(second_half(mid_a, ping_a, pong_a, full_a, bias_a, coef1, middle))
-        have_sides(A4)
-        all_rows(second_half(mid_a, ping_a, pong_a, full_a, bias_a, coef1, sides))
-        writing(full_a, 0, 0, 0, N).start()
+
+    def adjoint_sides():
+        @pl.when(role == 1)
+        def _():
+            have_sides(A4)
+            all_rows(second_half(mid_a, ping_a, pong_a, full_a, bias_a, coef1, sides))
+            writing(full_a, 0, 0, 0, N).start()
 
     def leave_final(i):
+        if i == 1:
+            adjoint_sides()
         if i == 2:
             writing(final, 1, 0, 6, N).start()
         if i == 3:

time: 67.2 us -> 67.3 us (level)
  no operation moved by 1% of the time
where the time goes in v4:
time: 67.3 us; the launch traced here: 66.9 us
  Pallas kernels  64.1 us (95%)
  local copies, waits for them, and re-layouts  2.7 us (4%)
    pallas_call x1, Pallas kernels, per_device(): pl.pallas_call(kernel, out_shape=jax.ShapeDtypeStruct((2, N, N, 8, 128),...  64.1 us
    reshape x1, local copies, waits for them, and re-layouts, per_device(): return result.reshape(1, 2, N, N, 1024)  2.7 us

profile of v4, /device:TPU:65, one launch (start us, length us, event | category | flops | bytes accessed | tf_op | source)
XLA Modules:
  0.0 66.9 jit_solution(13954672242698564052)
XLA Ops:
  0.0 64.1 %shard_map.46 = f32[2,16,16,8,128]{4,3,2,1,0:T(8,128)} custom-call(f32[16,16,1024]{2,1,0:T(8,128)} %temp_hbm.1, f32[16,16,1024]{2,1,0:T(8,128)} %visc_hbm.1, s32[16,16,1024]{2,1,0:T(8,128)} %pinned_hbm.1, f32[2,16,16,1024]{3,2,1,0:T(8,128)} %loads_hbm.1), custom_call_target="tpu_custom_call" | custom-call | tf_op jit(solution)/shard_map/pallas_call | solution.py:539
  64.2 2.7 %reshape.3 = f32[1,2,16,16,1024]{4,3,2,1,0:T(8,128)} reshape(f32[2,16,16,8,128]{4,3,2,1,0:T(8,128)} %shard_map.46) | data formatting | bytes 4194304 | tf_op jit(solution)/shard_map/reshape | solution.py:549
